TPU v7x, 32 devices: a whole 2x2x4 slice. The times are simulated.
32 devices in a mesh: row: 4 (over z), col: 8 (over y, x, core).
Axes of the slice: x: 2, y: 2, z: 4, core: 2. Of those that a mesh axis runs over, the one named last changes fastest.
Arguments:
- embeddings: bfloat16 [4096, 768], P(('row', 'col')), may hold values from -4 to 4
- neg_ids: int32 [4, 2048], P('row', 'col'), may hold values from 0 to 16383, as said below
- neg_counts: int32 [4], P('row'), may hold values from 256 to 2048, as said below
- index_rows: bfloat16 [16384, 768], P('row'), may hold values from -4 to 4
Outputs:
- row_loss: float32 [4096], P(('row', 'col'))
- grad: float32 [4096, 768], P(('row', 'col'))
Inputs may be any that keep to these rules, and one draw needn't show every extreme that they name: `neg_counts`: every entry lies within the range; some lists are full (2048) and some hold exactly 256 entries. Index shard of an id is id // 4096. Among the 256 slots of one device (neg_ids[b, c * 256 : (c + 1) * 256]) at most 128 ids belong to any one index shard, and in every such run exactly 128 belong to one of them.
All inputs are finite; a program needn't handle non-finite values.
Results may differ from a plain program's by a relative error of at most 0.00059.
Values may be sent and summed in bfloat16 or wider, within the bound.
A program may use at most 128 MiB of HBM per device.

v0:
```python
import jax
import jax.numpy as jnp
from jax import lax
from jax.sharding import PartitionSpec as P

D = 768


def per_device(embeddings, neg_ids, neg_counts, index_rows):
    scale = D ** (-0.5)
    n_col = lax.axis_size("col")
    shard_rows = embeddings.shape[0]
    width = embeddings.shape[1]
    row_id = lax.axis_index("row")
    col_id = lax.axis_index("col")
    queries = lax.all_gather(embeddings, "col", axis=0, tiled=True)
    keys = lax.all_gather(embeddings, "row", axis=0, tiled=True)
    query_count = queries.shape[0]
    key_count = keys.shape[0]
    requests = lax.all_gather(neg_ids, "row", axis=0, tiled=True)
    owned_count = index_rows.shape[0]
    slot_count = neg_ids.shape[1]
    local_ids = requests - row_id * owned_count
    owned = (local_ids >= 0) & (local_ids < owned_count)
    picked = jnp.take(index_rows, jnp.clip(local_ids, 0, owned_count - 1), axis=0)
    picked = jnp.where(owned[..., None], picked, jnp.zeros_like(picked))
    fetched = lax.psum_scatter(
        picked.astype(jnp.float32).astype(jnp.bfloat16), "row", scatter_dimension=0, tiled=True
    ).astype(jnp.float32)
    negatives = fetched[0].astype(jnp.bfloat16)
    row_glob = row_id * query_count + jnp.arange(query_count, dtype=jnp.int32)
    key_local = jnp.arange(key_count, dtype=jnp.int32)
    col_glob = (key_local // shard_rows * n_col + col_id) * shard_rows + key_local % shard_rows
    scores = jnp.dot(queries, keys.T, preferred_element_type=jnp.float32) * scale
    scores = jnp.where(row_glob[:, None] == col_glob[None, :], -jnp.inf, scores)
    slot_glob = col_id * slot_count + jnp.arange(slot_count, dtype=jnp.int32)
    hard = jnp.dot(queries, negatives.T, preferred_element_type=jnp.float32) * scale
    hard = jnp.where((slot_glob < neg_counts[0])[None, :], hard, -jnp.inf)
    local_top = jnp.maximum(jnp.max(scores, axis=1), jnp.max(hard, axis=1))
    top = lax.pmax(local_top, "col")
    partial_value = jnp.sum(jnp.exp(scores - top[:, None]), axis=1) + jnp.sum(
        jnp.exp(hard - top[:, None]), axis=1
    )
    total = lax.psum(partial_value, "col")
    lse = top + jnp.log(total)
    own_f = embeddings.astype(jnp.float32)
    partner = own_f.reshape(shard_rows // 2, 2, width)[:, ::-1].reshape(shard_rows, width)
    positive = jnp.sum(own_f * partner, axis=1) * scale
    own_lse = lax.dynamic_slice_in_dim(lse, col_id * shard_rows, shard_rows, 0)
    row_loss = own_lse - positive
    target = (jnp.bitwise_xor(row_glob, 1)[:, None] == col_glob[None, :]).astype(jnp.float32)
    probs_grad = (jnp.exp(scores - lse[:, None]) - target).astype(jnp.bfloat16)
    hard_probs = jnp.exp(hard - lse[:, None]).astype(jnp.bfloat16)
    term = jnp.dot(probs_grad, keys, preferred_element_type=jnp.float32)
    query_part = lax.psum_scatter(
        term + jnp.dot(hard_probs, negatives, preferred_element_type=jnp.float32),
        "col",
        scatter_dimension=0,
        tiled=True,
    )
    key_part = lax.psum_scatter(
        lax.dot_general(
            probs_grad, queries, (((0,), (0,)), ((), ())), preferred_element_type=jnp.float32
        ),
        "row",
        scatter_dimension=0,
        tiled=True,
    )
    grad = query_part + key_part
    return (row_loss, grad)


def solution(mesh):
    return jax.shard_map(
        per_device,
        mesh=mesh,
        in_specs=(P(("row", "col"), None), P("row", "col"), P("row"), P("row", None)),
        out_specs=(P(("row", "col")), P(("row", "col"), None)),
        check_vma=False,
    )
```

profile of v0, /device:TPU:0, one launch (start us, length us, event | category | flops | bytes accessed | tf_op | source)
XLA Modules:
  0.0 196.2 jit_solution(175145558935563326)
XLA Ops:
  8.0 0.0 all-gather.3.cloned.1.call-start
  8.0 0.7 all-gather.3.cloned.1.call-update
  8.7 0.0 reduce-scatter.4.cloned.1.call-start
  8.8 12.8 %all-gather = s32[4,1,256]{2,1,0:T(1,128)S(1)} all-gather(s32[1,1,256]{2,1,0:T(1,128)} %bitcast.31), channel_id=1, replica_groups=mesh['row'=4,'col'=8] {'row'}, dimensions={0}, use_global_device_ids=true | all-gather | bytes 5120 | tf_op jit(solution)/shard_map/all_gather | solution.py:20
  21.7 8.1 %gather_fusion = bf16[1024,768]{1,0:T(8,128)(2,1)S(1)} fusion(bf16[4096,768]{1,0:T(8,128)(2,1)} %param.7, s32[1024]{0:T(1024)S(1)} %broadcast_clamp_fusion), kind=kCustom, calls=%fused_computation | custom fusion | bytes 3149824 | tf_op jit(solution)/shard_map/jit(_take)/gather | solution.py:25
  29.8 0.0 copy-start
  29.8 1.4 select_select_fusion
  31.2 0.0 reduce-scatter.4.cloned.1.call-update
  31.2 0.0 reduce-scatter.8.cloned.1.call-start
  32.0 0.0 copy-done
  32.0 26.3 %all_gather.10 = bf16[512,768]{1,0:T(8,128)(2,1)S(1)} all-gather(bf16[128,768]{1,0:T(8,128)(2,1)S(1)} %copy-done), channel_id=1, replica_groups=mesh['row'=4,'col'=8] {'row'}, dimensions={0}, use_global_device_ids=true | all-gather | bytes 983040 | tf_op jit(solution)/shard_map/all_gather | solution.py:17
  58.3 0.0 copy-start.1
  58.3 0.0 all-gather.3.cloned.1.call-done
  58.3 2.7 %fusion.18 = (f32[1024]{0:T(1024)S(1)}, f32[1024,512]{0,1:T(8,128)S(1)}) fusion(bf16[1024,768]{1,0:T(8,128)(2,1)} %all-gather.3.cloned.1.call-done, bf16[512,768]{1,0:T(8,128)(2,1)S(1)} %all_gather.10, s32[512]{0:T(512)S(1)} %fusion.12, s32[1024]{0:T(1024)S(1)} %iota_add_fusion), kind=kOutput, calls=%fused_computation.43 | convolution fusion | flops 807402496 | bytes 4466688 | tf_op jit(solution)/shard_map/dot_general | solution.py:34
  61.0 0.0 copy-done.1
  61.0 12.1 %reduce-scatter.4.cloned.1.call-done = bf16[1,256,768]{2,1,0:T(8,128)(2,1)} async-done(((bf16[4,256,768]{2,1,0:T(8,128)(2,1)}), bf16[1,256,768]{2,1,0:T(8,128)(2,1)}) %reduce-scatter.4.cloned.1.call-update) | async-done | bytes 393232 | tf_op jit(solution)/shard_map/reduce_scatter | solution.py:27
  73.1 2.2 %fusion.19 = (f32[1024]{0:T(1024)S(1)}, f32[256,1024]{1,0:T(8,128)S(1)}) fusion(bf16[1024,768]{1,0:T(8,128)(2,1)} %all-gather.3.cloned.1.call-done, bf16[1,256,768]{2,1,0:T(8,128)(2,1)} %reduce-scatter.4.cloned.1.call-done, pred[256]{0:T(512)(128)(4,1)S(1)} %add_compare_fusion), kind=kOutput, calls=%fused_computation.44 | convolution fusion | flops 403438592 | bytes 3019008 | tf_op jit(solution)/shard_map/dot_general | solution.py:37
  75.3 14.0 %pmax.7 = f32[1024]{0:T(1024)S(1)} all-reduce(f32[1024]{0:T(1024)S(1)} %max.9), channel_id=1, replica_groups=mesh['row'=4,'col'=8] {'col'}, use_global_device_ids=true, to_apply=%region_3.4 | all-reduce | flops 1024 | bytes 8192 | tf_op jit(solution)/shard_map/pmax | solution.py:40
  89.2 0.2 exponential_reduce_fusion.1
  89.4 0.3 exponential_reduce_fusion
  89.7 11.8 %psum.7 = f32[1024]{0:T(1024)S(1)} all-reduce(f32[1024]{0:T(1024)S(1)} %add.93), channel_id=1, replica_groups=mesh['row'=4,'col'=8] {'col'}, use_global_device_ids=true, to_apply=%region_6.7 | all-reduce | flops 1024 | bytes 8192 | tf_op jit(solution)/shard_map/psum | solution.py:44
  101.5 3.8 %fusion.16 = f32[512,768]{1,0:T(8,128)} fusion(bf16[1024,768]{1,0:T(8,128)(2,1)} %all-gather.3.cloned.1.call-done, f32[1024,512]{0,1:T(8,128)S(1)} %get-tuple-element.3, s32[1024]{0:T(1024)S(1)} %broadcast_xor_fusion, f32[1024]{0:T(1024)S(1)} %log_add_fusion, s32[512]{0:T(512)S(1)} %fusion.12), kind=kOutput, calls=%fused_computation.41 | convolution fusion | flops 807927808 | bytes 5253120 | tf_op jit(solution)/shard_map/dot_general | solution.py:62
  105.3 0.0 reduce-scatter.8.cloned.1.call-update
  105.3 0.0 reduce-scatter.6.cloned.1.call-start
  105.4 0.0 copy-start.2
  105.4 2.3 %fusion.17 = f32[1024,768]{1,0:T(8,128)S(1)} fusion(bf16[512,768]{1,0:T(8,128)(2,1)} %copy-done.1, f32[1024,512]{0,1:T(8,128)S(1)} %get-tuple-element.3, s32[1024]{0:T(1024)S(1)} %broadcast_xor_fusion, f32[1024]{0:T(1024)S(1)} %log_add_fusion, s32[512]{0:T(512)S(1)} %fusion.12), kind=kOutput, calls=%fused_computation.42 | convolution fusion | flops 807927808 | bytes 6039552 | tf_op jit(solution)/shard_map/dot_general | solution.py:54
  107.7 0.0 copy-done.2
  107.7 2.3 %convolution_add_fusion = f32[1024,768]{1,0:T(8,128)} fusion(f32[1024,768]{1,0:T(8,128)S(1)} %fusion.17, f32[256,1024]{1,0:T(8,128)S(1)} %get-tuple-element.5, f32[1024]{0:T(1024)S(1)} %log_add_fusion, bf16[1,256,768]{2,1,0:T(8,128)(2,1)S(1)} %copy-done.2), kind=kOutput, calls=%fused_computation.4 | convolution fusion | flops 403963904 | bytes 7737344 | tf_op jit(solution)/shard_map/dot_general | solution.py:56
  110.0 0.0 reduce-scatter.6.cloned.1.call-update
  110.0 0.2 reshape.55
  110.2 1.1 rev.3
  111.4 0.3 reshape.56
  111.6 0.1 multiply_reduce_fusion
  111.8 0.6 multiply_subtract_fusion
  112.3 26.1 %reduce-scatter.8.cloned.1.call-done = f32[128,768]{1,0:T(8,128)} async-done(((f32[512,768]{1,0:T(8,128)}), f32[128,768]{1,0:T(8,128)}) %reduce-scatter.8.cloned.1.call-update) | async-done | bytes 393232 | tf_op jit(solution)/shard_map/reduce_scatter | solution.py:61
  138.4 48.2 %reduce-scatter.6.cloned.1.call-done = f32[128,768]{1,0:T(8,128)} async-done(((f32[1024,768]{1,0:T(8,128)}), f32[128,768]{1,0:T(8,128)}) %reduce-scatter.6.cloned.1.call-update) | async-done | bytes 393232 | tf_op jit(solution)/shard_map/reduce_scatter | solution.py:55
  186.7 1.9 add.97
  (14 shorter events, 0.1 us)
Async XLA Ops:
  8.0 50.3 %all-gather.3.cloned.1.call-start = ((), (), s32[]{:S(2)}) async-start(), calls=%async_computation.3 | async-start | bytes 1769472 | tf_op jit(solution)/shard_map/all_gather | solution.py:16
  8.7 64.4 %reduce-scatter.4.cloned.1.call-start = ((), (), s32[]{:S(2)}) async-start(), calls=%async_computation.4 | async-start | bytes 1966080 | tf_op jit(solution)/shard_map/reduce_scatter | solution.py:27
  29.8 2.2 %copy-start = (bf16[128,768]{1,0:T(8,128)(2,1)S(1)}, bf16[128,768]{1,0:T(8,128)(2,1)}, u32[]{:S(2)}) copy-start(bf16[128,768]{1,0:T(8,128)(2,1)} %param.4) | copy-start | bytes 589828
  31.2 107.2 %reduce-scatter.8.cloned.1.call-start = ((), (), s32[]{:S(2)}) async-start(), calls=%async_computation.6 | async-start | bytes 1966080 | tf_op jit(solution)/shard_map/reduce_scatter | solution.py:61
  58.3 2.7 %copy-start.1 = (bf16[512,768]{1,0:T(8,128)(2,1)}, bf16[512,768]{1,0:T(8,128)(2,1)S(1)}, u32[]{:S(2)}) copy-start(bf16[512,768]{1,0:T(8,128)(2,1)S(1)} %all_gather.10) | copy-start | bytes 2359300
  105.3 81.4 %reduce-scatter.6.cloned.1.call-start = ((), (), s32[]{:S(2)}) async-start(), calls=%async_computation.5 | async-start | bytes 3538944 | tf_op jit(solution)/shard_map/reduce_scatter | solution.py:55
  105.4 2.3 %copy-start.2 = (bf16[1,256,768]{2,1,0:T(8,128)(2,1)S(1)}, bf16[1,256,768]{2,1,0:T(8,128)(2,1)}, u32[]{:S(2)}) copy-start(bf16[1,256,768]{2,1,0:T(8,128)(2,1)} %reduce-scatter.4.cloned.1.call-done) | copy-start | bytes 1179652
Sparse Core Ops, SparseCore 0:
  10.7 28.4 all-gather.2
Sparse Core Ops, SparseCore 1:
  31.3 41.7 reduce-scatter.3
  105.4 33.0 reduce-scatter.7
  141.7 44.9 reduce-scatter.5
where the time goes:
time: 197 us; the launch traced here: 196 us
  waiting for transfers between devices  87.1 us (44%)
  blocking collectives  64.9 us (33%)
  between operations  16.5 us (8%)
  matrix products  13.3 us (7%)
  local copies, waits for them, and re-layouts  9.65 us (5%)
  other arithmetic  4.59 us (2%)
    reduce_scatter x1, waiting for transfers between devices, per_device(): lax.psum_scatter(term + jnp.dot(hard_probs, negatives, preferred_element_...  48.2 us
    all_gather x1, blocking collectives, per_device(): keys = lax.all_gather(embeddings, 'row', axis=0, tiled=True)  26.3 us
    reduce_scatter x1, waiting for transfers between devices, per_device(): lax.psum_scatter(lax.dot_general(probs_grad, queries, (((0,), (0,)), ((),...  26.1 us
    pmax x1, blocking collectives, per_device(): top = lax.pmax(local_top, 'col')  14 us
    all_gather x1, blocking collectives, per_device(): requests = lax.all_gather(neg_ids, 'row', axis=0, tiled=True)  12.8 us
    reduce_scatter x1, waiting for transfers between devices, per_device(): lax.psum_scatter(picked.astype(jnp.float32).astype(jnp.bfloat16), 'row',...  12.1 us
    psum x1, blocking collectives, per_device(): total = lax.psum(partial_value, 'col')  11.8 us
    gather x1, local copies, waits for them, and re-layouts, per_device(): jnp.take(index_rows, jnp.clip(local_ids, 0, owned_count - 1), axis=0)  8.07 us
  transfers between devices with their start and end apart: 4, of which 3 were waited for; matrix products, arithmetic and copies ran while one was open for 10% of the time, Pallas kernels for 0%

commit v1 on v0

--- a/solution.py
+++ b/solution.py
@@ -14,7 +14,12 @@
     row_id = lax.axis_index("row")
     col_id = lax.axis_index("col")
     queries = lax.all_gather(embeddings, "col", axis=0, tiled=True)
-    keys = lax.all_gather(embeddings, "row", axis=0, tiled=True)
+    ring = [embeddings]
+    for hop in range(3):
+        ring.append(lax.ppermute(ring[-1], "row", [(dev, (dev + 1) % 4) for dev in range(4)]))
+    keys = jnp.roll(
+        jnp.concatenate(ring[::-1], axis=0), (lax.axis_index("row") + 1) * ring[0].shape[0], axis=0
+    )
     query_count = queries.shape[0]
     key_count = keys.shape[0]
     requests = lax.all_gather(neg_ids, "row", axis=0, tiled=True)

time: 197 us -> 197 us (level)
  blocking collectives: 64.9 us -> 38.5 us
  waiting for transfers between devices: 87.1 us -> 107 us
  local copies, waits for them, and re-layouts: 9.65 us -> 16 us
    ppermute x0 -> x3, waiting for transfers between devices: none -> 31.4 us  [per_device(): lax.ppermute(ring[-1], 'row', [(dev, (dev + 1) % 4) for dev in range(4)])]
    all_gather x1 -> x0, blocking collectives: 26.3 us -> none  [per_device(): keys = lax.all_gather(embeddings, 'row', axis=0, tiled=True)]
    reduce_scatter x1, waiting for transfers between devices: 12.1 us -> 1.74 us  [per_device(): lax.psum_scatter(picked.astype(jnp.float32).astype(jnp.bfloat16), 'row',...]
    unnamed x8 -> x11, local copies, waits for them, and re-layouts: 0.02 us -> 5.72 us
  transfers between devices with their start and end apart: 4 -> 7, of which waited for: 3 -> 6; matrix products, arithmetic and copies ran while one was open for 10% -> 13% of each run, Pallas kernels for 0% -> 0%
where the time goes in v1:
time: 197 us
  waiting for transfers between devices  107 us (54%)
  blocking collectives  38.5 us (20%)
  between operations  16.5 us (8%)
  local copies, waits for them, and re-layouts  16 us (8%)
  matrix products  14.2 us (7%)
  other arithmetic  4.6 us (2%)
    reduce_scatter x1, waiting for transfers between devices, per_device(): lax.psum_scatter(term + jnp.dot(hard_probs, negatives, preferred_element_...  48.3 us
    ppermute x3, waiting for transfers between devices, per_device(): lax.ppermute(ring[-1], 'row', [(dev, (dev + 1) % 4) for dev in range(4)])  31.4 us
    reduce_scatter x1, waiting for transfers between devices, per_device(): lax.psum_scatter(lax.dot_general(probs_grad, queries, (((0,), (0,)), ((),...  24.7 us
    pmax x1, blocking collectives, per_device(): top = lax.pmax(local_top, 'col')  13.9 us
    all_gather x1, blocking collectives, per_device(): requests = lax.all_gather(neg_ids, 'row', axis=0, tiled=True)  12.8 us
    psum x1, blocking collectives, per_device(): total = lax.psum(partial_value, 'col')  11.8 us
    gather x1, local copies, waits for them, and re-layouts, per_device(): jnp.take(index_rows, jnp.clip(local_ids, 0, owned_count - 1), axis=0)  8.07 us
    unnamed x11, local copies, waits for them, and re-layouts  5.72 us
  transfers between devices with their start and end apart: 7, of which 6 were waited for; matrix products, arithmetic and copies ran while one was open for 13% of the time, Pallas kernels for 0%

profile of v1, /device:TPU:0, one launch (start us, length us, event | category | flops | bytes accessed | tf_op | source)
XLA Modules:
  0.0 196.9 jit_solution(15286123292843201838)
XLA Ops:
  8.0 0.0 all-gather.3.cloned.1.call-start
  8.0 0.7 all-gather.3.cloned.1.call-update
  8.7 0.0 reduce-scatter.4.cloned.1.call-start
  8.8 12.8 %all-gather = s32[4,1,256]{2,1,0:T(1,128)S(1)} all-gather(s32[1,1,256]{2,1,0:T(1,128)} %bitcast.31), channel_id=1, replica_groups=mesh['row'=4,'col'=8] {'row'}, dimensions={0}, use_global_device_ids=true | all-gather | bytes 5120 | tf_op jit(solution)/shard_map/all_gather | solution.py:25
  21.7 8.1 %gather_fusion = bf16[1024,768]{1,0:T(8,128)(2,1)S(1)} fusion(bf16[4096,768]{1,0:T(8,128)(2,1)} %param.7, s32[1024]{0:T(1024)S(1)} %broadcast_clamp_fusion), kind=kCustom, calls=%fused_computation | custom fusion | bytes 3149824 | tf_op jit(solution)/shard_map/jit(_take)/gather | solution.py:30
  29.8 1.4 select_select_fusion
  31.2 0.0 copy-start
  31.2 0.0 reduce-scatter.4.cloned.1.call-update
  31.2 0.0 reduce-scatter.8.cloned.1.call-start
  31.3 0.8 copy-done
  32.1 0.0 collective-permute-start
  32.8 7.1 %collective-permute-done = bf16[128,768]{1,0:T(8,128)(2,1)S(1)} collective-permute-done((bf16[128,768]{1,0:T(8,128)(2,1)S(1)}, bf16[128,768]{1,0:T(8,128)(2,1)S(1)}, u32[]{:S(2)}, u32[]{:S(2)}) %collective-permute-start) | collective-permute-done | bytes 196640 | tf_op jit(solution)/shard_map/ppermute | solution.py:19
  39.9 0.0 collective-permute-start.1
  40.0 12.2 %collective-permute-done.1 = bf16[128,768]{1,0:T(8,128)(2,1)S(1)} collective-permute-done((bf16[128,768]{1,0:T(8,128)(2,1)S(1)}, bf16[128,768]{1,0:T(8,128)(2,1)S(1)}, u32[]{:S(2)}, u32[]{:S(2)}) %collective-permute-start.1) | collective-permute-done | bytes 196640 | tf_op jit(solution)/shard_map/ppermute | solution.py:19
  52.1 0.0 collective-permute-start.2
  52.2 12.1 %collective-permute-done.2 = bf16[128,768]{1,0:T(8,128)(2,1)S(1)} collective-permute-done((bf16[128,768]{1,0:T(8,128)(2,1)S(1)}, bf16[128,768]{1,0:T(8,128)(2,1)S(1)}, u32[]{:S(2)}, u32[]{:S(2)}) %collective-permute-start.2) | collective-permute-done | bytes 196640 | tf_op jit(solution)/shard_map/ppermute | solution.py:19
  64.3 0.7 constant_dynamic-update-slice_fusion.7
  64.9 0.7 constant_dynamic-update-slice_fusion.6
  65.6 0.7 constant_dynamic-update-slice_fusion.5
  66.3 0.7 constant_dynamic-update-slice_fusion.4
  67.0 0.7 constant_dynamic-update-slice_fusion.3
  67.7 0.7 constant_dynamic-update-slice_fusion.2
  68.4 0.7 constant_dynamic-update-slice_fusion.1
  69.1 0.7 constant_dynamic-update-slice_fusion
  69.8 0.0 all-gather.3.cloned.1.call-done
  69.8 2.7 %fusion.22 = (f32[1024]{0:T(1024)S(1)}, f32[1024,512]{0,1:T(8,128)S(1)}) fusion(bf16[1024,768]{1,0:T(8,128)(2,1)} %all-gather.3.cloned.1.call-done, bf16[1024,768]{1,0:T(8,128)(2,1)} %constant_dynamic-update-slice_fusion, s32[]{:T(128)S(6)} %select_n.60, s32[512]{0:T(512)S(1)} %fusion.15, s32[1024]{0:T(1024)S(1)} %iota_add_fusion), kind=kOutput, calls=%fused_computation.55 | convolution fusion | flops 807402496 | bytes 4466692 | tf_op jit(solution)/shard_map/dot_general | solution.py:39
  72.5 1.7 reduce-scatter.4.cloned.1.call-done
  74.2 2.2 %fusion.23 = (f32[1024]{0:T(1024)S(1)}, f32[256,1024]{1,0:T(8,128)S(1)}) fusion(bf16[1024,768]{1,0:T(8,128)(2,1)} %all-gather.3.cloned.1.call-done, bf16[1,256,768]{2,1,0:T(8,128)(2,1)} %reduce-scatter.4.cloned.1.call-done, pred[256]{0:T(512)(128)(4,1)S(1)} %add_compare_fusion), kind=kOutput, calls=%fused_computation.56 | convolution fusion | flops 403438592 | bytes 3019008 | tf_op jit(solution)/shard_map/dot_general | solution.py:42
  76.4 13.9 %pmax.7 = f32[1024]{0:T(1024)S(1)} all-reduce(f32[1024]{0:T(1024)S(1)} %max.9), channel_id=1, replica_groups=mesh['row'=4,'col'=8] {'col'}, use_global_device_ids=true, to_apply=%region_3.4 | all-reduce | flops 1024 | bytes 8192 | tf_op jit(solution)/shard_map/pmax | solution.py:45
  90.3 0.2 exponential_reduce_fusion.1
  90.5 0.3 exponential_reduce_fusion
  90.8 11.8 %psum.7 = f32[1024]{0:T(1024)S(1)} all-reduce(f32[1024]{0:T(1024)S(1)} %add.109), channel_id=1, replica_groups=mesh['row'=4,'col'=8] {'col'}, use_global_device_ids=true, to_apply=%region_6.7 | all-reduce | flops 1024 | bytes 8192 | tf_op jit(solution)/shard_map/psum | solution.py:49
  102.6 3.8 %fusion.21 = f32[512,768]{1,0:T(8,128)} fusion(bf16[1024,768]{1,0:T(8,128)(2,1)} %all-gather.3.cloned.1.call-done, f32[1024,512]{0,1:T(8,128)S(1)} %get-tuple-element.3, s32[1024]{0:T(1024)S(1)} %broadcast_xor_fusion, f32[1024]{0:T(1024)S(1)} %log_add_fusion, s32[512]{0:T(512)S(1)} %fusion.15), kind=kOutput, calls=%fused_computation.54 | convolution fusion | flops 807927808 | bytes 5253120 | tf_op jit(solution)/shard_map/dot_general | solution.py:67
  106.4 0.0 reduce-scatter.8.cloned.1.call-update
  106.4 0.0 reduce-scatter.6.cloned.1.call-start
  106.5 1.6 fusion.3
  108.1 4.0 %convolution_add_fusion = f32[1024,768]{1,0:T(8,128)} fusion(f32[1024,768]{1,0:T(8,128)S(1)} %fusion.3, bf16[1024,768]{1,0:T(8,128)(2,1)} %constant_dynamic-update-slice_fusion, s32[]{:T(128)S(6)} %select_n.60, f32[1024,512]{0,1:T(8,128)S(1)} %get-tuple-element.3, s32[1024]{0:T(1024)S(1)} %broadcast_xor_fusion, f32[1024]{0:T(1024)S(1)} %log_add_fusion, ...), kind=kOutput, calls=%fused_computation.4 | convolution fusion | flops 808714240 | bytes 9185284 | tf_op jit(solution)/shard_map/dot_general | solution.py:59
  112.1 0.0 reduce-scatter.6.cloned.1.call-update
  112.1 0.2 reshape.55
  112.3 1.1 rev.3
  113.4 0.3 reshape.56
  113.7 0.1 multiply_reduce_fusion
  113.8 0.6 multiply_subtract_fusion
  114.4 24.7 %reduce-scatter.8.cloned.1.call-done = f32[128,768]{1,0:T(8,128)} async-done(((f32[512,768]{1,0:T(8,128)}), f32[128,768]{1,0:T(8,128)}) %reduce-scatter.8.cloned.1.call-update) | async-done | bytes 393232 | tf_op jit(solution)/shard_map/reduce_scatter | solution.py:66
  139.1 48.3 %reduce-scatter.6.cloned.1.call-done = f32[128,768]{1,0:T(8,128)} async-done(((f32[1024,768]{1,0:T(8,128)}), f32[128,768]{1,0:T(8,128)}) %reduce-scatter.6.cloned.1.call-update) | async-done | bytes 393232 | tf_op jit(solution)/shard_map/reduce_scatter | solution.py:60
  187.4 1.9 add.113
  (14 shorter events, 0.1 us)
Async XLA Ops:
  8.0 61.8 %all-gather.3.cloned.1.call-start = ((), (), s32[]{:S(2)}) async-start(), calls=%async_computation.3 | async-start | bytes 1769472 | tf_op jit(solution)/shard_map/all_gather | solution.py:16
  8.7 65.5 %reduce-scatter.4.cloned.1.call-start = ((), (), s32[]{:S(2)}) async-start(), calls=%async_computation.4 | async-start | bytes 1966080 | tf_op jit(solution)/shard_map/reduce_scatter | solution.py:32
  31.2 0.9 copy-start
  31.2 107.9 %reduce-scatter.8.cloned.1.call-start = ((), (), s32[]{:S(2)}) async-start(), calls=%async_computation.6 | async-start | bytes 1966080 | tf_op jit(solution)/shard_map/reduce_scatter | solution.py:66
  32.1 7.8 %collective-permute-start = (bf16[128,768]{1,0:T(8,128)(2,1)S(1)}, bf16[128,768]{1,0:T(8,128)(2,1)S(1)}, u32[]{:S(2)}, u32[]{:S(2)}) collective-permute-start(bf16[128,768]{1,0:T(8,128)(2,1)S(1)} %copy-done), channel_id=1, source_target_pairs={{0,8},{8,16},{16,24},{24,0},{1,9},{9,17},{17,25},{25,1},{2,10},{10... | collective-permute-start | bytes 589832 | tf_op jit(solution)/shard_map/ppermute | solution.py:19
  39.9 12.2 %collective-permute-start.1 = (bf16[128,768]{1,0:T(8,128)(2,1)S(1)}, bf16[128,768]{1,0:T(8,128)(2,1)S(1)}, u32[]{:S(2)}, u32[]{:S(2)}) collective-permute-start(bf16[128,768]{1,0:T(8,128)(2,1)S(1)} %collective-permute-done), channel_id=1, source_target_pairs={{0,8},{8,16},{16,24},{24,0},{1,9},{9,17},{17,25},{25,1},{2,10},{10... | collective-permute-start | bytes 589832 | tf_op jit(solution)/shard_map/ppermute | solution.py:19
  52.1 12.1 %collective-permute-start.2 = (bf16[128,768]{1,0:T(8,128)(2,1)S(1)}, bf16[128,768]{1,0:T(8,128)(2,1)S(1)}, u32[]{:S(2)}, u32[]{:S(2)}) collective-permute-start(bf16[128,768]{1,0:T(8,128)(2,1)S(1)} %collective-permute-done.1), channel_id=1, source_target_pairs={{0,8},{8,16},{16,24},{24,0},{1,9},{9,17},{17,25},{25,1},{2,10},{10... | collective-permute-start | bytes 589832 | tf_op jit(solution)/shard_map/ppermute | solution.py:19
  106.4 81.0 %reduce-scatter.6.cloned.1.call-start = ((), (), s32[]{:S(2)}) async-start(), calls=%async_computation.5 | async-start | bytes 3538944 | tf_op jit(solution)/shard_map/reduce_scatter | solution.py:60
Sparse Core Ops, SparseCore 0:
  10.7 28.3 all-gather.2
Sparse Core Ops, SparseCore 1:
  31.3 42.9 reduce-scatter.3
  106.5 32.5 reduce-scatter.7
  142.3 45.0 reduce-scatter.5
